TPU v7x, 32 devices: a whole 2x2x4 slice. The times are simulated.
32 devices in a mesh: pb: 16 (over z, x, core), ka: 2 (over y).
Axes of the slice: x: 2, y: 2, z: 4, core: 2. Of those that a mesh axis runs over, the one named last changes fastest.
Arguments:
- queries: bfloat16 [2048, 2048], P(('pb', 'ka')), may hold values from -8 to 8
- keys: bfloat16 [2048, 128], P(('ka', 'pb')), may hold values from -6 to 6
- values: bfloat16 [2048, 128], P(('ka', 'pb')), may hold values from -6 to 6
- query_pos: int32 [2048], replicated, may hold values from 0 to 2047, as said below
- key_pos: int32 [2048], replicated, may hold values from 0 to 2047, as said below
- block_mask: int32 [32, 32], replicated, may hold values from 0 to 1, as said below
Outputs:
- attended: bfloat16 [2048, 2048], P(('pb', 'ka'))
Inputs may be any that keep to these rules, and one draw needn't show every extreme that they name: `query_pos`: query tile u (rows u * 64 to (u + 1) * 64 - 1) holds 64 consecutive positions in increasing order, 0 + r * 64 onward, where the tiles' r are a permutation of 0 to 31. `key_pos`: key tile t (rows t * 64 to (t + 1) * 64 - 1) holds 64 consecutive positions in increasing order, r * 64 onward, where the tiles' r are a permutation of 0 to 31. `block_mask`: every query tile may attend to the key tile that holds position 0.
All inputs are finite; a program needn't handle non-finite values.
Results may differ from a plain program's by a relative error of at most 0.0015.
Values may be sent and summed in bfloat16 or wider, within the bound.
No kernel may reach another device: no remote copies, remote signals or barrier semaphores. Data moves between devices by JAX's collectives and lax.ppermute only.
A program may use at most 128 MiB of HBM per device.

v0:
```python
import jax
import jax.numpy as jnp
from jax import lax
from jax.sharding import PartitionSpec as P

NEG = -1e30


def tiles_per_piece(rows, tiles, k_rows):
    best = 1
    for count in range(1, tiles + 1):
        if tiles % count == 0 and rows * count * k_rows <= 3 * 2**20:
            best = count
    return best


def update(state, flat_queries, rows, heads, key_piece, value_piece, allowed):
    top, total, summed = state
    width = key_piece.shape[1]
    piece = key_piece.shape[0]
    scale = width ** (-0.5)
    scores = jnp.dot(flat_queries, key_piece.T, preferred_element_type=jnp.float32) * scale
    scores = scores.reshape(rows, heads, piece)
    masked = jnp.where(allowed[:, None, :], scores, NEG)
    new_top = jnp.maximum(top, jnp.max(masked, axis=-1))
    weights = jnp.where(allowed[:, None, :], jnp.exp(scores - new_top[..., None]), 0.0)
    factor = jnp.exp(top - new_top)
    total = total * factor + jnp.sum(weights, axis=-1)
    product = jnp.dot(
        weights.reshape(rows * heads, piece),
        value_piece.astype(jnp.float32),
        precision=lax.Precision.HIGHEST,
    )
    summed = summed * factor[..., None] + product.reshape(rows, heads, width)
    return (new_top, total, summed)


def start_state(rows, heads, width):
    return (
        jnp.full((rows, heads), NEG, jnp.float32),
        jnp.zeros((rows, heads), jnp.float32),
        jnp.zeros((rows, heads, width), jnp.float32),
    )


def attend(q_rows, q_pos, tile_ok, keys_all, values_all, k_pos, q_dev, k_dev, heads):
    rows = q_rows.shape[0]
    width = keys_all.shape[1]
    tiles = tile_ok.shape[1]
    per_piece = tiles_per_piece(rows * heads, tiles, k_dev)
    piece = per_piece * k_dev
    turns = tiles // per_piece
    flat_queries = q_rows.reshape(rows * heads, width)

    def one_turn(turn, state):
        start = (turn * piece).astype(jnp.int32)
        key_piece = lax.dynamic_slice_in_dim(keys_all, start, piece, 0)
        value_piece = lax.dynamic_slice_in_dim(values_all, start, piece, 0)
        pos_piece = lax.dynamic_slice_in_dim(k_pos, start, piece, 0)
        ok_piece = lax.dynamic_slice_in_dim(
            tile_ok, (turn * per_piece).astype(jnp.int32), per_piece, 1
        )
        ok_rows = jnp.repeat(jnp.repeat(ok_piece, q_dev, axis=0), k_dev, axis=1)
        allowed = (pos_piece[None, :] <= q_pos[:, None]) & (ok_rows > 0)
        return update(state, flat_queries, rows, heads, key_piece, value_piece, allowed)

    return lax.fori_loop(0, turns, one_turn, start_state(rows, heads, width))


def shards(queries, keys, values, query_pos, key_pos, block_mask):
    q_dev = queries.shape[0]
    k_dev = keys.shape[0]
    width = keys.shape[1]
    heads = queries.shape[1] // width
    n_pb = lax.axis_size("pb")
    n_ka = lax.axis_size("ka")
    block_idx = lax.axis_index("pb")
    key_idx = lax.axis_index("ka")
    q_block = lax.all_gather(queries, "ka", axis=0, tiled=True)
    keys_block, values_block = (
        lax.all_gather(keys, "pb", axis=0, tiled=True),
        lax.all_gather(values, "pb", axis=0, tiled=True),
    )
    rows = q_block.shape[0]
    span = keys_block.shape[0]
    q_pos = lax.dynamic_slice_in_dim(query_pos, block_idx * rows, rows, 0)
    k_pos = lax.dynamic_slice_in_dim(key_pos, key_idx * span, span, 0)
    tile_ok = lax.dynamic_slice(block_mask, (block_idx * n_ka, key_idx * n_pb), (n_ka, n_pb))
    top, total, summed = attend(
        q_block, q_pos, tile_ok, keys_block, values_block, k_pos, q_dev, k_dev, heads
    )
    overall = lax.pmax(top, "ka")
    factor = jnp.exp(top - overall)
    summed = (summed * factor[..., None]).reshape(rows, heads * width)
    total = total * factor
    mine, share = (
        lax.psum_scatter(summed, "ka", scatter_dimension=0, tiled=True),
        lax.psum_scatter(total, "ka", scatter_dimension=0, tiled=True),
    )
    result = mine.reshape(q_dev, heads, width) / share[..., None]
    return result.reshape(q_dev, heads * width).astype(jnp.bfloat16)


def solution(mesh):
    return jax.shard_map(
        shards,
        mesh=mesh,
        in_specs=(
            P(("pb", "ka"), None),
            P(("ka", "pb"), None),
            P(("ka", "pb"), None),
            P(),
            P(),
            P(),
        ),
        out_specs=P(("pb", "ka"), None),
        check_vma=False,
    )
```

profile of v0, /device:TPU:0, one launch (start us, length us, event | category | flops | bytes accessed | tf_op | source)
XLA Modules:
  0.0 117.5 jit_solution(1697706964040492435)
XLA Ops:
  6.5 0.8 dynamic-slice_compare_fusion
  7.3 0.1 copy.16
  7.4 0.1 broadcast_in_dim.58
  7.5 0.1 gt.17
  7.6 0.7 dynamic_slice.17
  8.3 0.8 dynamic_slice.18
  9.0 0.2 bitcast_and_fusion
  9.2 0.2 copy.17
  9.5 10.2 %all_gather.9 = bf16[128,2048]{1,0:T(8,128)(2,1)S(1)} all-gather(bf16[64,2048]{1,0:T(8,128)(2,1)} %param.6), channel_id=1, replica_groups=mesh['pb'=16,'ka'=2] {'ka'}, dimensions={0}, use_global_device_ids=true | all-gather | bytes 786432 | tf_op jit(solution)/shard_map/all_gather | solution.py:79
  19.7 0.2 reshape.77
  19.9 22.8 %all_gather.10 = bf16[1024,128]{1,0:T(8,128)(2,1)S(1)} all-gather(bf16[64,128]{1,0:T(8,128)(2,1)} %param.7), channel_id=1, replica_groups=mesh['pb'=16,'ka'=2] {'pb'}, dimensions={0}, use_global_device_ids=true | all-gather | bytes 278528 | tf_op jit(solution)/shard_map/all_gather | solution.py:81
  42.7 4.8 %fusion = (f32[2048]{0:T(1024)S(1)}, f32[2048,1024]{1,0:T(8,128)}) fusion(pred[128,1024]{1,0:T(8,128)(4,1)S(1)} %copy.17, bf16[2048,128]{1,0:T(8,128)(2,1)S(1)} %reshape.77, bf16[1024,128]{1,0:T(8,128)(2,1)S(1)} %all_gather.10), kind=kOutput, calls=%fused_computation.2 | convolution fusion | flops 543160320 | bytes 9314304 | tf_op jit(solution)/shard_map/while/body/eval_jaxpr/dot_general | solution.py:22
  47.5 0.1 max.17
  47.6 6.6 %fusion.4 = (f32[2048]{0:T(1024)S(1)}, f32[2048,1024]{1,0:T(8,128)}) fusion(f32[2048]{0:T(1024)S(1)} %broadcast_maximum_fusion, f32[2048,1024]{1,0:T(8,128)} %get-tuple-element.31, pred[128,1024]{1,0:T(8,128)(4,1)S(1)} %copy.17), kind=kLoop, calls=%fused_computation.15 | loop fusion | flops 8386560 | bytes 16924672 | tf_op jit(solution)/shard_map/while/body/eval_jaxpr/reduce_sum | solution.py:28
  54.2 0.1 reduce_sum.13
  54.3 8.9 %pmax.7 = f32[128,16]{1,0:T(8,128)S(1)} all-reduce(f32[128,16]{1,0:T(8,128)S(1)} %max.17), channel_id=1, replica_groups=mesh['pb'=16,'ka'=2] {'ka'}, use_global_device_ids=true, to_apply=%region_1.0 | all-reduce | flops 2048 | bytes 16384 | tf_op jit(solution)/shard_map/pmax | solution.py:92
  63.1 0.7 add_multiply_fusion
  63.8 0.0 reduce-scatter.3.cloned.1.call-start
  63.9 17.8 %all_gather.11 = bf16[1024,128]{1,0:T(8,128)(2,1)S(1)} all-gather(bf16[64,128]{1,0:T(8,128)(2,1)S(1)} %copy-done), channel_id=1, replica_groups=mesh['pb'=16,'ka'=2] {'pb'}, dimensions={0}, use_global_device_ids=true | all-gather | bytes 278528 | tf_op jit(solution)/shard_map/all_gather | solution.py:82
  81.7 6.3 %fusion.1 = f32[128,16,128]{2,1,0:T(8,128)S(1)} fusion(f32[128,16,1024]{2,1,0:T(8,128)} %bitcast.26, f32[128,16]{1,0:T(8,128)S(1)} %get-tuple-element.26, f32[128,16]{1,0:T(8,128)S(1)} %get-tuple-element.29, bf16[1024,128]{1,0:T(8,128)(2,1)S(1)} %all_gather.11), kind=kOutput, calls=%fused_computation.4 | convolution fusion | flops 3221749760 | bytes 9715712 | tf_op jit(solution)/shard_map/while/body/eval_jaxpr/dot_general | solution.py:29
  88.0 1.3 %copy.22 = f32[16,8,16,128]{3,1,2,0:T(8,128)} copy(f32[16,8,16,128]{3,2,1,0:T(8,128)S(1)} %bitcast.27) | data formatting | bytes 2097152
  89.4 18.3 %reduce-scatter.3.cloned.1.call-done = f32[64,2048]{1,0:T(8,128)} async-done(((f32[128,2048]{1,0:T(8,128)}), f32[64,2048]{1,0:T(8,128)}) %reduce-scatter.3.cloned.1.call-update) | async-done | bytes 524304 | tf_op jit(solution)/shard_map/reduce_scatter | solution.py:97
  107.7 0.9 div.11
  108.7 2.0 %fusion.2 = bf16[64,2048]{1,0:T(8,128)(2,1)} fusion(f32[64,2048]{1,0:T(8,128)} %reduce-scatter.3.cloned.1.call-done, f32[8,8,16,128]{3,2,1,0:T(8,128)S(1)} %bitcast.29), kind=kLoop, calls=%fused_computation.7 | loop fusion | flops 262144 | bytes 1310720 | tf_op jit(solution)/shard_map/convert_element_type | solution.py:101
  (7 shorter events, 0.1 us)
Async XLA Ops:
  6.5 82.8 %reduce-scatter.5.cloned.1.call-start = ((), (), s32[]{:S(2)}) async-start(), calls=%async_computation.3 | async-start | bytes 98304 | tf_op jit(solution)/shard_map/reduce_scatter | solution.py:98
  47.6 16.3 %copy-start = (bf16[64,128]{1,0:T(8,128)(2,1)S(1)}, bf16[64,128]{1,0:T(8,128)(2,1)}, u32[]{:S(2)}) copy-start(bf16[64,128]{1,0:T(8,128)(2,1)} %param.8) | copy-start | bytes 49156
  63.8 43.9 %reduce-scatter.3.cloned.1.call-start = ((), (), s32[]{:S(2)}) async-start(), calls=%async_computation.2 | async-start | bytes 1572864 | tf_op jit(solution)/shard_map/reduce_scatter | solution.py:97
Sparse Core Ops, SparseCore 0:
  63.9 6.1 reduce-scatter.4
  89.5 18.2 reduce-scatter.2
where the time goes:
time: 118 us; the launch traced here: 117 us
  blocking collectives  59.7 us (51%)
  waiting for transfers between devices  18.4 us (16%)
  between operations  13.5 us (11%)
  matrix products  11.1 us (9%)
  other arithmetic  10.2 us (9%)
  local copies, waits for them, and re-layouts  4.64 us (4%)
    all_gather x1, blocking collectives, shards(): lax.all_gather(keys, 'pb', axis=0, tiled=True)  22.8 us
    reduce_scatter x1, waiting for transfers between devices, shards(): lax.psum_scatter(summed, 'ka', scatter_dimension=0, tiled=True)  18.3 us
    all_gather x1, blocking collectives, shards(): lax.all_gather(values, 'pb', axis=0, tiled=True)  17.8 us
    all_gather x1, blocking collectives, shards(): q_block = lax.all_gather(queries, 'ka', axis=0, tiled=True)  10.2 us
    pmax x1, blocking collectives, shards(): overall = lax.pmax(top, 'ka')  8.85 us
    reduce_sum x1, other arithmetic, update(): total = total * factor + jnp.sum(weights, axis=-1)  6.58 us
    dot_general x1, matrix products, update(): jnp.dot(weights.reshape(rows * heads, piece), value_piece.astype(jnp.floa...  6.27 us
    dot_general x1, matrix products, update(): jnp.dot(flat_queries, key_piece.T, preferred_element_type=jnp.float32)  4.82 us
  transfers between devices with their start and end apart: 2, of which 1 were waited for; matrix products, arithmetic and copies ran while one was open for 6% of the time, Pallas kernels for 0%

commit v1 on v0

v1 whole, which is shorter than its diff:
```python
import functools
import math

import jax
import jax.numpy as jnp
from jax import lax
from jax.experimental import pallas as pl
from jax.experimental.pallas import tpu as pltpu
from jax.sharding import PartitionSpec as P

NEG = -1e30
NEVER = -(2**30)
VMEM = pl.BlockSpec(memory_space=pltpu.VMEM)
SMEM = pl.BlockSpec(memory_space=pltpu.SMEM)
PARAMS = pltpu.CompilerParams(vmem_limit_bytes=48 * 2**20)


def swap(x, step, n_devices):
    return lax.ppermute(x, ("pb", "ka"), [(i, i ^ step) for i in range(n_devices)])


def step_groups(n_pb, n_ka):
    core = n_ka
    bits = [1 << b for b in range((n_pb * n_ka).bit_length() - 1)]
    bits.remove(core)
    groups = []
    while bits:
        pair, bits = bits[:2], bits[2:]
        groups.insert(0, [pair[0], pair[1], pair[0] ^ pair[1]] if len(pair) == 2 else pair)
    far = [[g[1], g[2], g[0]] if len(g) == 3 else g for g in groups[:-1]]
    return far + groups[-1:], core


def plan_kernel(n_pb, n_ka, tiles, q_pos, k_pos, mask, q_ref, qs_ref, reach_ref):
    q_dev, columns = q_ref.shape
    width = qs_ref.shape[1]
    k_dev = k_pos.shape[0] // len(tiles)
    pb, ka = lax.axis_index("pb"), lax.axis_index("ka")
    me = pb * n_ka + ka
    mine = ka * n_pb + pb
    for h in range(columns // width):
        qs_ref[h * q_dev : (h + 1) * q_dev, :] = q_ref[:, h * width : (h + 1) * width]
    first = q_pos[me * q_dev]
    for row, step in enumerate(tiles):
        tile = mine ^ step
        reach = jnp.where(mask[me, tile] == 1, first - k_pos[tile * k_dev], NEVER)
        reach_ref[row : row + 1, :] = jnp.full((1, reach_ref.shape[1]), reach, jnp.int32)


def plan(queries, query_pos, key_pos, block_mask, n_pb, n_ka, tiles, width):
    q_dev, columns = queries.shape
    return pl.pallas_call(
        functools.partial(plan_kernel, n_pb, n_ka, tiles),
        out_shape=(
            jax.ShapeDtypeStruct((q_dev * columns // width, width), queries.dtype),
            jax.ShapeDtypeStruct((len(tiles), 2 * q_dev), jnp.int32),
        ),
        in_specs=[SMEM, SMEM, SMEM, VMEM],
        out_specs=(VMEM, VMEM),
        compiler_params=PARAMS,
        name="plan",
    )(query_pos, key_pos, block_mask, queries)


def part_kernel(rows, q_dev, lanes, has_state, last, *refs):
    refs = list(refs)
    n = len(rows)
    qs_ref, reach_ref = refs[:2]
    pieces, refs = refs[2 : 2 + n], refs[2 + n :]
    if has_state:
        (top_in, acc_in), refs = refs[:2], refs[2:]
    if last:
        out_ref, scores, out_vmem, sems = refs
    else:
        top_out, acc_out, scores = refs
    width = qs_ref.shape[1]
    factor = width ** (-0.5) * math.log2(math.e)
    keys = pieces[0].shape[0]
    blocks = qs_ref.shape[0] // lanes
    pair = reach_ref.shape[1]
    k_dev = keys // (rows[0][1] - rows[0][0])
    ahead = lax.broadcasted_iota(jnp.int32, (k_dev, pair), 0)
    ahead = ahead - lax.broadcasted_iota(jnp.int32, (k_dev, pair), 1) % q_dev
    ones = jnp.ones((16, keys), jnp.bfloat16)
    turned = [jnp.concatenate([piece[:, width:].T, ones], 0) for piece in pieces]

    def score(block, j, q):
        s = lax.dot_general(
            pieces[j][:, :width], q, (((1,), (1,)), ((), ())), preferred_element_type=jnp.float32
        )
        top = None
        for i, row in enumerate(range(*rows[j])):
            allowed = ahead <= reach_ref[row : row + 1, :]
            allowed = jnp.concatenate([allowed] * (lanes // pair), 1)
            tile = jnp.where(allowed, s[i * k_dev : (i + 1) * k_dev], NEG)
            scores[block % 2, j, i * k_dev : (i + 1) * k_dev, :] = tile
            high = jnp.max(tile.reshape(k_dev // 8, 8, lanes), axis=0)
            top = high if top is None else jnp.maximum(top, high)
        return top

    def queries_of(block):
        return qs_ref[block * lanes : (block + 1) * lanes, :]

    def score_all(block):
        q = queries_of(block)
        return functools.reduce(jnp.maximum, [score(block, j, q) for j in range(n)])

    high = score_all(0)
    copies = []
    for block in range(blocks):
        columns = slice(block * lanes, (block + 1) * lanes)
        top = jnp.max(high, axis=0, keepdims=True)
        if has_state:
            old = top_in[:1, columns]
            top = jnp.maximum(top, old)
        high = acc = None
        for j in range(n):
            if block + 1 < blocks:
                more = score(block + 1, j, queries_of(block + 1))
                high = more if high is None else jnp.maximum(high, more)
            p = jnp.exp2((scores[block % 2, j] - top) * factor)
            coarse = p.astype(jnp.bfloat16)
            fine = (p - coarse.astype(jnp.float32)).astype(jnp.bfloat16)
            more = jnp.dot(turned[j], coarse, preferred_element_type=jnp.float32)
            more += jnp.dot(turned[j], fine, preferred_element_type=jnp.float32)
            acc = more if acc is None else acc + more
        if has_state:
            acc = acc + acc_in[:, columns] * jnp.exp2((old - top) * factor)
        if not last:
            top_out[:, columns] = jnp.broadcast_to(top, (8, lanes))
            acc_out[:, columns] = acc
            continue
        result = (acc[:width] * (1.0 / acc[width : width + 1])).astype(jnp.bfloat16).T
        heads = lanes // q_dev
        for i in range(heads):
            h = block * heads + i
            out_vmem[:, h * width : (h + 1) * width] = result[i * q_dev : (i + 1) * q_dev]
        where = (slice(None), slice(block * heads * width, (block + 1) * heads * width))
        copy = pltpu.make_async_copy(out_vmem.at[where], out_ref.at[where], sems.at[block])
        copy.start()
        copies.append(copy)
    for copy in copies:
        copy.wait()


def part(qs, reach, pieces, rows, q_dev, state=None, last=False):
    total, width = qs.shape
    lanes = 4 * q_dev
    keys = pieces[0].shape[0]
    scores = pltpu.VMEM((2, len(pieces), keys, lanes), jnp.float32)
    if last:
        shape = (q_dev, total // q_dev * width)
        out_shape, out_specs = jax.ShapeDtypeStruct(shape, jnp.bfloat16), pl.BlockSpec(memory_space=pl.ANY)
        scratch = [
            scores,
            pltpu.VMEM(shape, jnp.bfloat16),
            pltpu.SemaphoreType.DMA((total // lanes,)),
        ]
    else:
        out_shape = (
            jax.ShapeDtypeStruct((8, total), jnp.float32),
            jax.ShapeDtypeStruct((width + 16, total), jnp.float32),
        )
        out_specs = (VMEM, VMEM)
        scratch = [scores]
    args = [qs, reach, *pieces, *(state or ())]
    n_keys = keys * len(pieces)
    return pl.pallas_call(
        functools.partial(part_kernel, rows, q_dev, lanes, state is not None, last),
        out_shape=out_shape,
        in_specs=[VMEM] * len(args),
        out_specs=out_specs,
        scratch_shapes=scratch,
        compiler_params=PARAMS,
        cost_estimate=pl.CostEstimate(
            flops=8 * total * width * n_keys, bytes_accessed=4 * n_keys * width, transcendentals=total * n_keys
        ),
        name="part_last" if last else "part",
    )(*args)


def shards(n_pb, n_ka, queries, keys, values, query_pos, key_pos, block_mask):
    q_dev, width = queries.shape[0], keys.shape[1]
    n_devices = n_pb * n_ka
    groups, core = step_groups(n_pb, n_ka)

    def send(x, step):
        return swap(x, step, n_devices)

    x, steps = jnp.concatenate([keys, values], 1), [0]
    for group in groups[:-1]:
        x = jnp.concatenate([x] + [send(x, step) for step in group], 0)
        steps = [s ^ g for g in [0] + group for s in steps]
    n = len(steps)
    last = [0] + groups[-1]
    steps = [s ^ g ^ c for c in (0, core) for g in last for s in steps]
    tiles = [(s % n_ka) * n_pb + s // n_ka for s in steps]
    qs, reach = plan(queries, query_pos, key_pos, block_mask, n_pb, n_ka, tiles, width)
    x, qs, reach = lax.optimization_barrier((x, qs, reach))

    mine = [x] + [send(x, step) for step in groups[-1]]
    m = len(mine)
    rows = [(j * n, (j + 1) * n) for j in range(2 * m)]

    def add(state, some, last=False):
        pieces = [piece for piece, _ in some]
        return part(qs, reach, pieces, [rows[j] for _, j in some], q_dev, state, last)

    def after(arrays, state):
        return lax.optimization_barrier((arrays, state))

    state = add(None, [(x, 0), (send(x, core), m)])
    near, late = mine[1:-1], mine[-1]
    if near:
        near, state = after(near, state)
        others = [send(y, core) for y in near]
        state = add(state, [(y, 1 + j) for j, y in enumerate(near)])
    late, state = after(late, state)
    other = send(late, core)
    if near:
        state = add(state, [(y, m + 1 + j) for j, y in enumerate(others)])
    return add(state, [(late, m - 1), (other, 2 * m - 1)], last=True)


def solution(mesh):
    n_pb, n_ka = mesh.shape["pb"], mesh.shape["ka"]
    return jax.shard_map(
        functools.partial(shards, n_pb, n_ka),
        mesh=mesh,
        in_specs=(
            P(("pb", "ka"), None),
            P(("ka", "pb"), None),
            P(("ka", "pb"), None),
            P(),
            P(),
            P(),
        ),
        out_specs=P(("pb", "ka"), None),
        check_vma=False,
    )
```

time: 118 us -> 24.2 us (0.21)
  blocking collectives: 59.7 us -> 0 us
  between operations: 13.5 us -> 0.09 us
  waiting for transfers between devices: 18.4 us -> 5.68 us
  matrix products: 11.1 us -> 0 us
  other arithmetic: 10.2 us -> 0.01 us
  starting transfers between devices: 0.04 us -> 9.82 us
  Pallas kernels: 0 us -> 6.56 us
  local copies, waits for them, and re-layouts: 4.64 us -> 1.71 us
    all_gather x3 -> x0, blocking collectives: 50.8 us -> none  [the longest x1 22.8 us: shards(): lax.all_gather(keys, 'pb', axis=0, tiled=True)]
    reduce_scatter x2 -> x0, waiting for transfers between devices: 18.4 us -> none  [the longest x1 18.3 us: shards(): lax.psum_scatter(summed, 'ka', scatter_dimension=0, tiled=True)]
    dot_general x2 -> x0, matrix products: 11.1 us -> none  [the longest x1 6.27 us: update(): jnp.dot(weights.reshape(rows * heads, piece), value_piece.astype(jnp.floa...]
    ppermute x0 -> x10, starting transfers between devices: none -> 9.82 us  [swap(): lax.ppermute(x, ('pb', 'ka'), [(i, i ^ step) for i in range(n_devices)])]
    pmax x1 -> x0, blocking collectives: 8.85 us -> none  [shards(): overall = lax.pmax(top, 'ka')]
    reduce_sum x1 -> x0, other arithmetic: 6.58 us -> none  [update(): total = total * factor + jnp.sum(weights, axis=-1)]
    pallas_call x0 -> x5, Pallas kernels: none -> 6.56 us  [the longest x4 5.34 us: part(): pl.pallas_call(functools.partial(part_kernel, rows, q_dev, lanes, state i...]
    ppermute x0 -> x10, waiting for transfers between devices: none -> 5.68 us  [swap(): lax.ppermute(x, ('pb', 'ka'), [(i, i ^ step) for i in range(n_devices)])]
  transfers between devices with their start and end apart: 2 -> 10, of which waited for: 1 -> 5; matrix products, arithmetic and copies ran while one was open for 6% -> 0% of each run, Pallas kernels for 0% -> 19%
where the time goes in v1:
time: 24.2 us; the launch traced here: 23.9 us
  starting transfers between devices  9.82 us (41%)
  Pallas kernels  6.56 us (27%)
  waiting for transfers between devices  5.68 us (23%)
  local copies, waits for them, and re-layouts  1.71 us (7%)
    ppermute x10, starting transfers between devices, swap(): lax.ppermute(x, ('pb', 'ka'), [(i, i ^ step) for i in range(n_devices)])  9.82 us
    ppermute x10, waiting for transfers between devices, swap(): lax.ppermute(x, ('pb', 'ka'), [(i, i ^ step) for i in range(n_devices)])  5.68 us
    pallas_call x4, Pallas kernels, part(): pl.pallas_call(functools.partial(part_kernel, rows, q_dev, lanes, state i...  5.34 us
    unnamed x11, local copies, waits for them, and re-layouts  1.7 us
    pallas_call x1, Pallas kernels, plan(): pl.pallas_call(functools.partial(plan_kernel, n_pb, n_ka, tiles), out_sha...  1.22 us
  transfers between devices with their start and end apart: 10, of which 5 were waited for; matrix products, arithmetic and copies ran while one was open for 0% of the time, Pallas kernels for 19%

profile of v1, /device:TPU:0, one launch (start us, length us, event | category | flops | bytes accessed | tf_op | source)
XLA Modules:
  0.0 23.9 jit_solution(6755996972984004801)
XLA Ops:
  0.0 0.7 %constant_dynamic-update-slice_fusion.1 = bf16[64,256]{1,0:T(8,128)(2,1)S(1)} fusion(bf16[64,128]{1,0:T(8,128)(2,1)} %param.7), kind=kLoop, calls=%fused_computation.2 | loop fusion | bytes 32768
  0.7 0.0 copy-start.3
  0.8 4.1 %collective-permute-start = (bf16[64,256]{1,0:T(8,128)(2,1)S(1)}, bf16[64,256]{1,0:T(8,128)(2,1)S(1)}, u32[]{:S(2)}, u32[]{:S(2)}) collective-permute-start(bf16[64,256]{1,0:T(8,128)(2,1)S(1)} %constant_dynamic-update-slice_fusion), channel_id=1, source_target_pairs={{0,16},{1,17},{2,18},{3,19},{4,20},{5,21},{6,22},{7,23},{8,24},{9,... | collective-permute-start | bytes 98312 | tf_op jit(solution)/shard_map/ppermute | solution.py:19
  4.9 1.3 %collective-permute-start.1 = (bf16[64,256]{1,0:T(8,128)(2,1)S(1)}, bf16[64,256]{1,0:T(8,128)(2,1)S(1)}, u32[]{:S(2)}, u32[]{:S(2)}) collective-permute-start(bf16[64,256]{1,0:T(8,128)(2,1)S(1)} %constant_dynamic-update-slice_fusion), channel_id=1, source_target_pairs={{0,24},{1,25},{2,26},{3,27},{4,28},{5,29},{6,30},{7,31},{8,16},{9,... | collective-permute-start | bytes 98312 | tf_op jit(solution)/shard_map/ppermute | solution.py:19
  6.2 0.2 collective-permute-start.2
  6.5 0.9 %copy-done = bf16[64,2048]{1,0:T(8,128)(2,1)S(1)} copy-done((bf16[64,2048]{1,0:T(8,128)(2,1)S(1)}, bf16[64,2048]{1,0:T(8,128)(2,1)}, u32[]{:S(2)}) %copy-start) | copy-done | bytes 262168
  7.4 1.2 %plan.1 = (bf16[1024,128]{1,0:T(8,128)(2,1)S(1)}, s32[32,128]{1,0:T(8,128)S(1)}) custom-call(s32[2048]{0:T(1024)S(1)} %copy-done.2, s32[2048]{0:T(1024)S(1)} %copy-done.3, s32[32,32]{1,0:T(8,128)S(1)} %copy-done.1, bf16[64,2048]{1,0:T(8,128)(2,1)S(1)} %copy-done), custom_call_target="tpu_custom_call" | custom-call | tf_op jit(solution)/shard_map/plan/pallas_call | solution.py:52
  8.6 0.0 collective-permute-done
  8.7 1.9 %collective-permute-done.1 = bf16[64,256]{1,0:T(8,128)(2,1)S(1)} collective-permute-done((bf16[64,256]{1,0:T(8,128)(2,1)S(1)}, bf16[64,256]{1,0:T(8,128)(2,1)S(1)}, u32[]{:S(2)}, u32[]{:S(2)}) %collective-permute-start.1) | collective-permute-done | bytes 32800 | tf_op jit(solution)/shard_map/ppermute | solution.py:19
  10.6 0.1 collective-permute-start.6
  10.7 1.6 %collective-permute-start.4 = (bf16[256,256]{1,0:T(8,128)(2,1)S(1)}, bf16[256,256]{1,0:T(8,128)(2,1)S(1)}, u32[]{:S(2)}, u32[]{:S(2)}) collective-permute-start(bf16[256,256]{1,0:T(8,128)(2,1)S(1)} %pad_maximum_fusion.refs_2_), channel_id=1, source_target_pairs={{0,1},{1,0},{2,3},{3,2},{4,5},{5,4},{6,7},{7,6},{8,9},{9,8},{10,11... | collective-permute-start | bytes 393224 | tf_op jit(solution)/shard_map/ppermute | solution.py:19
  12.3 1.5 %collective-permute-start.5 = (bf16[256,256]{1,0:T(8,128)(2,1)S(1)}, bf16[256,256]{1,0:T(8,128)(2,1)S(1)}, u32[]{:S(2)}, u32[]{:S(2)}) collective-permute-start(bf16[256,256]{1,0:T(8,128)(2,1)S(1)} %pad_maximum_fusion.refs_2_), channel_id=1, source_target_pairs={{0,4},{1,5},{2,6},{3,7},{4,0},{5,1},{6,2},{7,3},{8,12},{9,13},{10,... | collective-permute-start | bytes 393224 | tf_op jit(solution)/shard_map/ppermute | solution.py:19
  13.8 0.5 %collective-permute-start.3 = (bf16[256,256]{1,0:T(8,128)(2,1)S(1)}, bf16[256,256]{1,0:T(8,128)(2,1)S(1)}, u32[]{:S(2)}, u32[]{:S(2)}) collective-permute-start(bf16[256,256]{1,0:T(8,128)(2,1)S(1)} %pad_maximum_fusion.refs_2_), channel_id=1, source_target_pairs={{0,5},{1,4},{2,7},{3,6},{4,1},{5,0},{6,3},{7,2},{8,13},{9,12},{10,... | collective-permute-start | bytes 393224 | tf_op jit(solution)/shard_map/ppermute | solution.py:19
  14.2 0.0 collective-permute-done.6.refs_3_
  14.2 1.1 %part.3 = (f32[8,1024]{1,0:T(8,128)S(1)}, f32[144,1024]{1,0:T(8,128)S(1)}) custom-call(bf16[1024,128]{1,0:T(8,128)(2,1)S(1)} %get-tuple-element.25.refs_0_, s32[32,128]{1,0:T(8,128)S(1)} %get-tuple-element.26.refs_1_, bf16[256,256]{1,0:T(8,128)(2,1)S(1)} %pad_maximum_fusion.refs_2_, bf16[256,256]{1,0:T(8,128)(2,1)S(1)} %collective-permute-done.6.refs_3_), custom_call_target="tpu_custom_call" | custom-call | flops 536870912 | bytes 262144 | tf_op jit(solution)/shard_map/part/pallas_call | solution.py:168
  15.3 1.3 %collective-permute-done.4.refs_2_ = bf16[256,256]{1,0:T(8,128)(2,1)S(1)} collective-permute-done((bf16[256,256]{1,0:T(8,128)(2,1)S(1)}, bf16[256,256]{1,0:T(8,128)(2,1)S(1)}, u32[]{:S(2)}, u32[]{:S(2)}) %collective-permute-start.4) | collective-permute-done | bytes 131104 | tf_op jit(solution)/shard_map/ppermute | solution.py:19
  16.6 2.0 %collective-permute-done.5.refs_3_ = bf16[256,256]{1,0:T(8,128)(2,1)S(1)} collective-permute-done((bf16[256,256]{1,0:T(8,128)(2,1)S(1)}, bf16[256,256]{1,0:T(8,128)(2,1)S(1)}, u32[]{:S(2)}, u32[]{:S(2)}) %collective-permute-start.5) | collective-permute-done | bytes 131104 | tf_op jit(solution)/shard_map/ppermute | solution.py:19
  18.6 0.5 %collective-permute-start.9 = (bf16[256,256]{1,0:T(8,128)(2,1)S(1)}, bf16[256,256]{1,0:T(8,128)(2,1)S(1)}, u32[]{:S(2)}, u32[]{:S(2)}) collective-permute-start(bf16[256,256]{1,0:T(8,128)(2,1)S(1)} %collective-permute-done.5.refs_3_), channel_id=1, source_target_pairs={{0,2},{1,3},{2,0},{3,1},{4,6},{5,7},{6,4},{7,5},{8,10},{9,11},{10,... | collective-permute-start | bytes 393224 | tf_op jit(solution)/shard_map/ppermute | solution.py:19
  19.1 1.2 %part.4 = (f32[8,1024]{1,0:T(8,128)S(1)}, f32[144,1024]{1,0:T(8,128)S(1)}) custom-call(bf16[1024,128]{1,0:T(8,128)(2,1)S(1)} %get-tuple-element.25.refs_0_, s32[32,128]{1,0:T(8,128)S(1)} %get-tuple-element.26.refs_1_, bf16[256,256]{1,0:T(8,128)(2,1)S(1)} %collective-permute-done.4.refs_2_, bf16[256,256]{1,0:T(8,128)(2,1)S(1)} %collective-permute-done.5.refs_3_, ...), custom_call_target="tpu_custom_call" | custom-call | flops 536870912 | bytes 262144 | tf_op jit(solution)/shard_map/part/pallas_call | solution.py:168
  20.3 0.3 %collective-permute-done.3.refs_2_ = bf16[256,256]{1,0:T(8,128)(2,1)S(1)} collective-permute-done((bf16[256,256]{1,0:T(8,128)(2,1)S(1)}, bf16[256,256]{1,0:T(8,128)(2,1)S(1)}, u32[]{:S(2)}, u32[]{:S(2)}) %collective-permute-start.3) | collective-permute-done | bytes 131104 | tf_op jit(solution)/shard_map/ppermute | solution.py:19
  20.6 0.0 collective-permute-done.9.refs_3_
  20.6 1.2 %part.5 = (f32[8,1024]{1,0:T(8,128)S(1)}, f32[144,1024]{1,0:T(8,128)S(1)}) custom-call(bf16[1024,128]{1,0:T(8,128)(2,1)S(1)} %get-tuple-element.25.refs_0_, s32[32,128]{1,0:T(8,128)S(1)} %get-tuple-element.26.refs_1_, bf16[256,256]{1,0:T(8,128)(2,1)S(1)} %collective-permute-done.8.refs_2_, bf16[256,256]{1,0:T(8,128)(2,1)S(1)} %collective-permute-done.9.refs_3_, ...), custom_call_target="tpu_custom_call" | custom-call | flops 536870912 | bytes 262144 | tf_op jit(solution)/shard_map/part/pallas_call | solution.py:168
  21.8 0.2 collective-permute-done.7.refs_3_
  21.9 1.9 %part_last.1 = bf16[64,2048]{1,0:T(8,128)(2,1)} custom-call(bf16[1024,128]{1,0:T(8,128)(2,1)S(1)} %get-tuple-element.25.refs_0_, s32[32,128]{1,0:T(8,128)S(1)} %get-tuple-element.26.refs_1_, bf16[256,256]{1,0:T(8,128)(2,1)S(1)} %collective-permute-done.3.refs_2_, bf16[256,256]{1,0:T(8,128)(2,1)S(1)} %collective-permute-done.7.refs_3_, ...), custom_call_target="tpu_custom_call" | custom-call | flops 536870912 | bytes 262144 | tf_op jit(solution)/shard_map/part_last/pallas_call | solution.py:168
  (14 shorter events, 0.0 us)
Async XLA Ops:
  0.0 0.7 %copy-start.4 = (bf16[64,128]{1,0:T(8,128)(2,1)S(1)}, bf16[64,128]{1,0:T(8,128)(2,1)}, u32[]{:S(2)}) copy-start(bf16[64,128]{1,0:T(8,128)(2,1)} %param.8) | copy-start | bytes 49156
  0.7 5.7 %copy-start.1 = (s32[32,32]{1,0:T(8,128)S(1)}, s32[32,32]{1,0:T(8,128)}, u32[]{:S(2)}) copy-start(s32[32,32]{1,0:T(8,128)} %mask.1) | copy-start | bytes 12292
  0.7 5.7 %copy-start.2 = (s32[2048]{0:T(1024)S(1)}, s32[2048]{0:T(1024)}, u32[]{:S(2)}) copy-start(s32[2048]{0:T(1024)} %q_pos.1) | copy-start | bytes 24580
  0.7 5.7 %copy-start.3 = (s32[2048]{0:T(1024)S(1)}, s32[2048]{0:T(1024)}, u32[]{:S(2)}) copy-start(s32[2048]{0:T(1024)} %k_pos.1) | copy-start | bytes 24580
  0.8 7.9 %collective-permute-start = (bf16[64,256]{1,0:T(8,128)(2,1)S(1)}, bf16[64,256]{1,0:T(8,128)(2,1)S(1)}, u32[]{:S(2)}, u32[]{:S(2)}) collective-permute-start(bf16[64,256]{1,0:T(8,128)(2,1)S(1)} %constant_dynamic-update-slice_fusion), channel_id=1, source_target_pairs={{0,16},{1,17},{2,18},{3,19},{4,20},{5,21},{6,22},{7,23},{8,24},{9,... | collective-permute-start | bytes 98312 | tf_op jit(solution)/shard_map/ppermute | solution.py:19
  4.9 5.7 %collective-permute-start.1 = (bf16[64,256]{1,0:T(8,128)(2,1)S(1)}, bf16[64,256]{1,0:T(8,128)(2,1)S(1)}, u32[]{:S(2)}, u32[]{:S(2)}) collective-permute-start(bf16[64,256]{1,0:T(8,128)(2,1)S(1)} %constant_dynamic-update-slice_fusion), channel_id=1, source_target_pairs={{0,24},{1,25},{2,26},{3,27},{4,28},{5,29},{6,30},{7,31},{8,16},{9,... | collective-permute-start | bytes 98312 | tf_op jit(solution)/shard_map/ppermute | solution.py:19
  6.2 4.4 %collective-permute-start.2 = (bf16[64,256]{1,0:T(8,128)(2,1)S(1)}, bf16[64,256]{1,0:T(8,128)(2,1)S(1)}, u32[]{:S(2)}, u32[]{:S(2)}) collective-permute-start(bf16[64,256]{1,0:T(8,128)(2,1)S(1)} %constant_dynamic-update-slice_fusion), channel_id=1, source_target_pairs={{0,8},{1,9},{2,10},{3,11},{4,12},{5,13},{6,14},{7,15},{8,0},{9,1},... | collective-permute-start | bytes 98312 | tf_op jit(solution)/shard_map/ppermute | solution.py:19
  6.5 1.0 %copy-start = (bf16[64,2048]{1,0:T(8,128)(2,1)S(1)}, bf16[64,2048]{1,0:T(8,128)(2,1)}, u32[]{:S(2)}) copy-start(bf16[64,2048]{1,0:T(8,128)(2,1)} %q_ref.1) | copy-start | bytes 786436
  10.6 3.6 %collective-permute-start.6 = (bf16[256,256]{1,0:T(8,128)(2,1)S(1)}, bf16[256,256]{1,0:T(8,128)(2,1)S(1)}, u32[]{:S(2)}, u32[]{:S(2)}) collective-permute-start(bf16[256,256]{1,0:T(8,128)(2,1)S(1)} %pad_maximum_fusion.refs_2_), channel_id=1, source_target_pairs={{0,2},{1,3},{2,0},{3,1},{4,6},{5,7},{6,4},{7,5},{8,10},{9,11},{10,... | collective-permute-start | bytes 393224 | tf_op jit(solution)/shard_map/ppermute | solution.py:19
  10.7 5.9 %collective-permute-start.4 = (bf16[256,256]{1,0:T(8,128)(2,1)S(1)}, bf16[256,256]{1,0:T(8,128)(2,1)S(1)}, u32[]{:S(2)}, u32[]{:S(2)}) collective-permute-start(bf16[256,256]{1,0:T(8,128)(2,1)S(1)} %pad_maximum_fusion.refs_2_), channel_id=1, source_target_pairs={{0,1},{1,0},{2,3},{3,2},{4,5},{5,4},{6,7},{7,6},{8,9},{9,8},{10,11... | collective-permute-start | bytes 393224 | tf_op jit(solution)/shard_map/ppermute | solution.py:19
  12.3 6.3 %collective-permute-start.5 = (bf16[256,256]{1,0:T(8,128)(2,1)S(1)}, bf16[256,256]{1,0:T(8,128)(2,1)S(1)}, u32[]{:S(2)}, u32[]{:S(2)}) collective-permute-start(bf16[256,256]{1,0:T(8,128)(2,1)S(1)} %pad_maximum_fusion.refs_2_), channel_id=1, source_target_pairs={{0,4},{1,5},{2,6},{3,7},{4,0},{5,1},{6,2},{7,3},{8,12},{9,13},{10,... | collective-permute-start | bytes 393224 | tf_op jit(solution)/shard_map/ppermute | solution.py:19
  13.8 6.8 %collective-permute-start.3 = (bf16[256,256]{1,0:T(8,128)(2,1)S(1)}, bf16[256,256]{1,0:T(8,128)(2,1)S(1)}, u32[]{:S(2)}, u32[]{:S(2)}) collective-permute-start(bf16[256,256]{1,0:T(8,128)(2,1)S(1)} %pad_maximum_fusion.refs_2_), channel_id=1, source_target_pairs={{0,5},{1,4},{2,7},{3,6},{4,1},{5,0},{6,3},{7,2},{8,13},{9,12},{10,... | collective-permute-start | bytes 393224 | tf_op jit(solution)/shard_map/ppermute | solution.py:19
  18.6 2.0 %collective-permute-start.8 = (bf16[256,256]{1,0:T(8,128)(2,1)S(1)}, bf16[256,256]{1,0:T(8,128)(2,1)S(1)}, u32[]{:S(2)}, u32[]{:S(2)}) collective-permute-start(bf16[256,256]{1,0:T(8,128)(2,1)S(1)} %collective-permute-done.4.refs_2_), channel_id=1, source_target_pairs={{0,2},{1,3},{2,0},{3,1},{4,6},{5,7},{6,4},{7,5},{8,10},{9,11},{10,... | collective-permute-start | bytes 393224 | tf_op jit(solution)/shard_map/ppermute | solution.py:19
  18.6 2.0 %collective-permute-start.9 = (bf16[256,256]{1,0:T(8,128)(2,1)S(1)}, bf16[256,256]{1,0:T(8,128)(2,1)S(1)}, u32[]{:S(2)}, u32[]{:S(2)}) collective-permute-start(bf16[256,256]{1,0:T(8,128)(2,1)S(1)} %collective-permute-done.5.refs_3_), channel_id=1, source_target_pairs={{0,2},{1,3},{2,0},{3,1},{4,6},{5,7},{6,4},{7,5},{8,10},{9,11},{10,... | collective-permute-start | bytes 393224 | tf_op jit(solution)/shard_map/ppermute | solution.py:19
  20.6 1.3 %collective-permute-start.7 = (bf16[256,256]{1,0:T(8,128)(2,1)S(1)}, bf16[256,256]{1,0:T(8,128)(2,1)S(1)}, u32[]{:S(2)}, u32[]{:S(2)}) collective-permute-start(bf16[256,256]{1,0:T(8,128)(2,1)S(1)} %collective-permute-done.3.refs_2_), channel_id=1, source_target_pairs={{0,2},{1,3},{2,0},{3,1},{4,6},{5,7},{6,4},{7,5},{8,10},{9,11},{10,... | collective-permute-start | bytes 393224 | tf_op jit(solution)/shard_map/ppermute | solution.py:19

commit v2 on v1

--- a/solution.py
+++ b/solution.py
@@ -93,32 +93,26 @@
             allowed = ahead <= reach_ref[row : row + 1, :]
             allowed = jnp.concatenate([allowed] * (lanes // pair), 1)
             tile = jnp.where(allowed, s[i * k_dev : (i + 1) * k_dev], NEG)
-            scores[block % 2, j, i * k_dev : (i + 1) * k_dev, :] = tile
+            scores[block, j, i * k_dev : (i + 1) * k_dev, :] = tile
             high = jnp.max(tile.reshape(k_dev // 8, 8, lanes), axis=0)
             top = high if top is None else jnp.maximum(top, high)
         return top
 
-    def queries_of(block):
-        return qs_ref[block * lanes : (block + 1) * lanes, :]
-
     def score_all(block):
-        q = queries_of(block)
+        q = qs_ref[block * lanes : (block + 1) * lanes, :]
         return functools.reduce(jnp.maximum, [score(block, j, q) for j in range(n)])
 
-    high = score_all(0)
+    highs = [score_all(block) for block in range(blocks)]
     copies = []
     for block in range(blocks):
         columns = slice(block * lanes, (block + 1) * lanes)
-        top = jnp.max(high, axis=0, keepdims=True)
+        top = jnp.max(highs[block], axis=0, keepdims=True)
         if has_state:
             old = top_in[:1, columns]
             top = jnp.maximum(top, old)
-        high = acc = None
+        acc = None
         for j in range(n):
-            if block + 1 < blocks:
-                more = score(block + 1, j, queries_of(block + 1))
-                high = more if high is None else jnp.maximum(high, more)
-            p = jnp.exp2((scores[block % 2, j] - top) * factor)
+            p = jnp.exp2((scores[block, j] - top) * factor)
             coarse = p.astype(jnp.bfloat16)
             fine = (p - coarse.astype(jnp.float32)).astype(jnp.bfloat16)
             more = jnp.dot(turned[j], coarse, preferred_element_type=jnp.float32)
@@ -147,7 +141,7 @@
     total, width = qs.shape
     lanes = 4 * q_dev
     keys = pieces[0].shape[0]
-    scores = pltpu.VMEM((2, len(pieces), keys, lanes), jnp.float32)
+    scores = pltpu.VMEM((total // lanes, len(pieces), keys, lanes), jnp.float32)
     if last:
         shape = (q_dev, total // q_dev * width)
         out_shape, out_specs = jax.ShapeDtypeStruct(shape, jnp.bfloat16), pl.BlockSpec(memory_space=pl.ANY)
@@ -209,17 +203,19 @@
     def after(arrays, state):
         return lax.optimization_barrier((arrays, state))
 
-    state = add(None, [(x, 0), (send(x, core), m)])
+    state = add(None, [(x, 0)])
     near, late = mine[1:-1], mine[-1]
     if near:
-        near, state = after(near, state)
-        others = [send(y, core) for y in near]
+        near[0], state = after(near[0], state)
+    others = [send(y, core) for y in near]
+    other = send(x, core)
+    if near:
         state = add(state, [(y, 1 + j) for j, y in enumerate(near)])
     late, state = after(late, state)
-    other = send(late, core)
-    if near:
-        state = add(state, [(y, m + 1 + j) for j, y in enumerate(others)])
-    return add(state, [(late, m - 1), (other, 2 * m - 1)], last=True)
+    last = send(late, core)
+    some = [(other, m)] + [(y, m + 1 + j) for j, y in enumerate(others)] + [(late, m - 1)]
+    state = add(state, some)
+    return add(state, [(last, 2 * m - 1)], last=True)
 
 
 def solution(mesh):

time: 24.2 us -> 23.6 us (0.975)
  waiting for transfers between devices: 5.68 us -> 5.12 us
  starting transfers between devices: 9.82 us -> 9.46 us
  Pallas kernels: 6.56 us -> 6.81 us
    ppermute x10, waiting for transfers between devices: 5.68 us -> 5.12 us  [swap(): lax.ppermute(x, ('pb', 'ka'), [(i, i ^ step) for i in range(n_devices)])]
    ppermute x10, starting transfers between devices: 9.82 us -> 9.46 us  [swap(): lax.ppermute(x, ('pb', 'ka'), [(i, i ^ step) for i in range(n_devices)])]
    pallas_call x4, Pallas kernels: 5.34 us -> 5.59 us  [part(): pl.pallas_call(functools.partial(part_kernel, rows, q_dev, lanes, state i...]
  transfers between devices with their start and end apart: 10 -> 10, of which waited for: 5 -> 4; matrix products, arithmetic and copies ran while one was open for 0% -> 0% of each run, Pallas kernels for 19% -> 23%
where the time goes in v2:
time: 23.6 us; the launch traced here: 23.2 us
  starting transfers between devices  9.46 us (40%)
  Pallas kernels  6.81 us (29%)
  waiting for transfers between devices  5.12 us (22%)
  local copies, waits for them, and re-layouts  1.71 us (7%)
    ppermute x10, starting transfers between devices, swap(): lax.ppermute(x, ('pb', 'ka'), [(i, i ^ step) for i in range(n_devices)])  9.46 us
    pallas_call x4, Pallas kernels, part(): pl.pallas_call(functools.partial(part_kernel, rows, q_dev, lanes, state i...  5.59 us
    ppermute x10, waiting for transfers between devices, swap(): lax.ppermute(x, ('pb', 'ka'), [(i, i ^ step) for i in range(n_devices)])  5.12 us
    unnamed x11, local copies, waits for them, and re-layouts  1.7 us
    pallas_call x1, Pallas kernels, plan(): pl.pallas_call(functools.partial(plan_kernel, n_pb, n_ka, tiles), out_sha...  1.22 us
  transfers between devices with their start and end apart: 10, of which 4 were waited for; matrix products, arithmetic and copies ran while one was open for 0% of the time, Pallas kernels for 23%

profile of v2, /device:TPU:0, one launch (start us, length us, event | category | flops | bytes accessed | tf_op | source)
XLA Modules:
  0.0 23.2 jit_solution(17957524727702313767)
XLA Ops:
  0.0 0.7 %constant_dynamic-update-slice_fusion.1 = bf16[64,256]{1,0:T(8,128)(2,1)S(1)} fusion(bf16[64,128]{1,0:T(8,128)(2,1)} %param.7), kind=kLoop, calls=%fused_computation.2 | loop fusion | bytes 32768
  0.7 0.0 copy-start.3
  0.8 4.1 %collective-permute-start = (bf16[64,256]{1,0:T(8,128)(2,1)S(1)}, bf16[64,256]{1,0:T(8,128)(2,1)S(1)}, u32[]{:S(2)}, u32[]{:S(2)}) collective-permute-start(bf16[64,256]{1,0:T(8,128)(2,1)S(1)} %constant_dynamic-update-slice_fusion), channel_id=1, source_target_pairs={{0,16},{1,17},{2,18},{3,19},{4,20},{5,21},{6,22},{7,23},{8,24},{9,... | collective-permute-start | bytes 98312 | tf_op jit(solution)/shard_map/ppermute | solution.py:19
  4.9 1.3 %collective-permute-start.1 = (bf16[64,256]{1,0:T(8,128)(2,1)S(1)}, bf16[64,256]{1,0:T(8,128)(2,1)S(1)}, u32[]{:S(2)}, u32[]{:S(2)}) collective-permute-start(bf16[64,256]{1,0:T(8,128)(2,1)S(1)} %constant_dynamic-update-slice_fusion), channel_id=1, source_target_pairs={{0,24},{1,25},{2,26},{3,27},{4,28},{5,29},{6,30},{7,31},{8,16},{9,... | collective-permute-start | bytes 98312 | tf_op jit(solution)/shard_map/ppermute | solution.py:19
  6.2 0.2 collective-permute-start.2
  6.5 0.9 %copy-done = bf16[64,2048]{1,0:T(8,128)(2,1)S(1)} copy-done((bf16[64,2048]{1,0:T(8,128)(2,1)S(1)}, bf16[64,2048]{1,0:T(8,128)(2,1)}, u32[]{:S(2)}) %copy-start) | copy-done | bytes 262168
  7.4 1.2 %plan.1 = (bf16[1024,128]{1,0:T(8,128)(2,1)S(1)}, s32[32,128]{1,0:T(8,128)S(1)}) custom-call(s32[2048]{0:T(1024)S(1)} %copy-done.2, s32[2048]{0:T(1024)S(1)} %copy-done.3, s32[32,32]{1,0:T(8,128)S(1)} %copy-done.1, bf16[64,2048]{1,0:T(8,128)(2,1)S(1)} %copy-done), custom_call_target="tpu_custom_call" | custom-call | tf_op jit(solution)/shard_map/plan/pallas_call | solution.py:52
  8.7 1.9 %collective-permute-done.1 = bf16[64,256]{1,0:T(8,128)(2,1)S(1)} collective-permute-done((bf16[64,256]{1,0:T(8,128)(2,1)S(1)}, bf16[64,256]{1,0:T(8,128)(2,1)S(1)}, u32[]{:S(2)}, u32[]{:S(2)}) %collective-permute-start.1) | collective-permute-done | bytes 32800 | tf_op jit(solution)/shard_map/ppermute | solution.py:19
  10.6 0.0 collective-permute-done.2
  10.6 1.6 %collective-permute-start.4 = (bf16[256,256]{1,0:T(8,128)(2,1)S(1)}, bf16[256,256]{1,0:T(8,128)(2,1)S(1)}, u32[]{:S(2)}, u32[]{:S(2)}) collective-permute-start(bf16[256,256]{1,0:T(8,128)(2,1)S(1)} %pad_maximum_fusion.refs_2_), channel_id=1, source_target_pairs={{0,1},{1,0},{2,3},{3,2},{4,5},{5,4},{6,7},{7,6},{8,9},{9,8},{10,11... | collective-permute-start | bytes 393224 | tf_op jit(solution)/shard_map/ppermute | solution.py:19
  12.2 1.5 %collective-permute-start.5 = (bf16[256,256]{1,0:T(8,128)(2,1)S(1)}, bf16[256,256]{1,0:T(8,128)(2,1)S(1)}, u32[]{:S(2)}, u32[]{:S(2)}) collective-permute-start(bf16[256,256]{1,0:T(8,128)(2,1)S(1)} %pad_maximum_fusion.refs_2_), channel_id=1, source_target_pairs={{0,4},{1,5},{2,6},{3,7},{4,0},{5,1},{6,2},{7,3},{8,12},{9,13},{10,... | collective-permute-start | bytes 393224 | tf_op jit(solution)/shard_map/ppermute | solution.py:19
  13.7 0.5 %collective-permute-start.3 = (bf16[256,256]{1,0:T(8,128)(2,1)S(1)}, bf16[256,256]{1,0:T(8,128)(2,1)S(1)}, u32[]{:S(2)}, u32[]{:S(2)}) collective-permute-start(bf16[256,256]{1,0:T(8,128)(2,1)S(1)} %pad_maximum_fusion.refs_2_), channel_id=1, source_target_pairs={{0,5},{1,4},{2,7},{3,6},{4,1},{5,0},{6,3},{7,2},{8,13},{9,12},{10,... | collective-permute-start | bytes 393224 | tf_op jit(solution)/shard_map/ppermute | solution.py:19
  14.2 0.8 %part.3 = (f32[8,1024]{1,0:T(8,128)S(1)}, f32[144,1024]{1,0:T(8,128)S(1)}) custom-call(bf16[1024,128]{1,0:T(8,128)(2,1)S(1)} %get-tuple-element.24.refs_0_, s32[32,128]{1,0:T(8,128)S(1)} %get-tuple-element.25.refs_1_, bf16[256,256]{1,0:T(8,128)(2,1)S(1)} %pad_maximum_fusion.refs_2_), custom_call_target="tpu_custom_call" | custom-call | flops 268435456 | bytes 131072 | tf_op jit(solution)/shard_map/part/pallas_call | solution.py:162
  15.0 1.9 %collective-permute-done.4.refs_2_ = bf16[256,256]{1,0:T(8,128)(2,1)S(1)} collective-permute-done((bf16[256,256]{1,0:T(8,128)(2,1)S(1)}, bf16[256,256]{1,0:T(8,128)(2,1)S(1)}, u32[]{:S(2)}, u32[]{:S(2)}) %collective-permute-start.4) | collective-permute-done | bytes 131104 | tf_op jit(solution)/shard_map/ppermute | solution.py:19
  16.9 0.3 %collective-permute-done.5.refs_3_ = bf16[256,256]{1,0:T(8,128)(2,1)S(1)} collective-permute-done((bf16[256,256]{1,0:T(8,128)(2,1)S(1)}, bf16[256,256]{1,0:T(8,128)(2,1)S(1)}, u32[]{:S(2)}, u32[]{:S(2)}) %collective-permute-start.5) | collective-permute-done | bytes 131104 | tf_op jit(solution)/shard_map/ppermute | solution.py:19
  17.2 0.2 collective-permute-start.9
  17.4 1.2 %part.4 = (f32[8,1024]{1,0:T(8,128)S(1)}, f32[144,1024]{1,0:T(8,128)S(1)}) custom-call(bf16[1024,128]{1,0:T(8,128)(2,1)S(1)} %get-tuple-element.24.refs_0_, s32[32,128]{1,0:T(8,128)S(1)} %get-tuple-element.25.refs_1_, bf16[256,256]{1,0:T(8,128)(2,1)S(1)} %collective-permute-done.4.refs_2_, bf16[256,256]{1,0:T(8,128)(2,1)S(1)} %collective-permute-done.5.refs_3_, ...), custom_call_target="tpu_custom_call" | custom-call | flops 536870912 | bytes 262144 | tf_op jit(solution)/shard_map/part/pallas_call | solution.py:162
  18.6 1.0 %collective-permute-done.3.refs_5_ = bf16[256,256]{1,0:T(8,128)(2,1)S(1)} collective-permute-done((bf16[256,256]{1,0:T(8,128)(2,1)S(1)}, bf16[256,256]{1,0:T(8,128)(2,1)S(1)}, u32[]{:S(2)}, u32[]{:S(2)}) %collective-permute-start.3) | collective-permute-done | bytes 131104 | tf_op jit(solution)/shard_map/ppermute | solution.py:19
  19.6 0.0 collective-permute-start.6
  19.6 0.0 collective-permute-done.7.refs_2_
  19.6 0.0 collective-permute-done.8.refs_3_
  19.6 2.1 %part.5 = (f32[8,1024]{1,0:T(8,128)S(1)}, f32[144,1024]{1,0:T(8,128)S(1)}) custom-call(bf16[1024,128]{1,0:T(8,128)(2,1)S(1)} %get-tuple-element.24.refs_0_, s32[32,128]{1,0:T(8,128)S(1)} %get-tuple-element.25.refs_1_, bf16[256,256]{1,0:T(8,128)(2,1)S(1)} %collective-permute-done.7.refs_2_, bf16[256,256]{1,0:T(8,128)(2,1)S(1)} %collective-permute-done.8.refs_3_, ...), custom_call_target="tpu_custom_call" | custom-call | flops 1073741824 | bytes 524288 | tf_op jit(solution)/shard_map/part/pallas_call | solution.py:162
  21.6 0.0 collective-permute-done.6.refs_2_
  21.6 1.6 %part_last.1 = bf16[64,2048]{1,0:T(8,128)(2,1)} custom-call(bf16[1024,128]{1,0:T(8,128)(2,1)S(1)} %get-tuple-element.24.refs_0_, s32[32,128]{1,0:T(8,128)S(1)} %get-tuple-element.25.refs_1_, bf16[256,256]{1,0:T(8,128)(2,1)S(1)} %collective-permute-done.6.refs_2_, f32[8,1024]{1,0:T(8,128)S(1)} %get-tuple-element.37.refs_3_, ...), custom_call_target="tpu_custom_call" | custom-call | flops 268435456 | bytes 131072 | tf_op jit(solution)/shard_map/part_last/pallas_call | solution.py:162
  (14 shorter events, 0.0 us)
Async XLA Ops:
  0.0 0.7 %copy-start.4 = (bf16[64,128]{1,0:T(8,128)(2,1)S(1)}, bf16[64,128]{1,0:T(8,128)(2,1)}, u32[]{:S(2)}) copy-start(bf16[64,128]{1,0:T(8,128)(2,1)} %param.8) | copy-start | bytes 49156
  0.7 5.7 %copy-start.1 = (s32[32,32]{1,0:T(8,128)S(1)}, s32[32,32]{1,0:T(8,128)}, u32[]{:S(2)}) copy-start(s32[32,32]{1,0:T(8,128)} %mask.1) | copy-start | bytes 12292
  0.7 5.7 %copy-start.2 = (s32[2048]{0:T(1024)S(1)}, s32[2048]{0:T(1024)}, u32[]{:S(2)}) copy-start(s32[2048]{0:T(1024)} %q_pos.1) | copy-start | bytes 24580
  0.7 5.7 %copy-start.3 = (s32[2048]{0:T(1024)S(1)}, s32[2048]{0:T(1024)}, u32[]{:S(2)}) copy-start(s32[2048]{0:T(1024)} %k_pos.1) | copy-start | bytes 24580
  0.8 7.9 %collective-permute-start = (bf16[64,256]{1,0:T(8,128)(2,1)S(1)}, bf16[64,256]{1,0:T(8,128)(2,1)S(1)}, u32[]{:S(2)}, u32[]{:S(2)}) collective-permute-start(bf16[64,256]{1,0:T(8,128)(2,1)S(1)} %constant_dynamic-update-slice_fusion), channel_id=1, source_target_pairs={{0,16},{1,17},{2,18},{3,19},{4,20},{5,21},{6,22},{7,23},{8,24},{9,... | collective-permute-start | bytes 98312 | tf_op jit(solution)/shard_map/ppermute | solution.py:19
  4.9 5.7 %collective-permute-start.1 = (bf16[64,256]{1,0:T(8,128)(2,1)S(1)}, bf16[64,256]{1,0:T(8,128)(2,1)S(1)}, u32[]{:S(2)}, u32[]{:S(2)}) collective-permute-start(bf16[64,256]{1,0:T(8,128)(2,1)S(1)} %constant_dynamic-update-slice_fusion), channel_id=1, source_target_pairs={{0,24},{1,25},{2,26},{3,27},{4,28},{5,29},{6,30},{7,31},{8,16},{9,... | collective-permute-start | bytes 98312 | tf_op jit(solution)/shard_map/ppermute | solution.py:19
  6.2 4.4 %collective-permute-start.2 = (bf16[64,256]{1,0:T(8,128)(2,1)S(1)}, bf16[64,256]{1,0:T(8,128)(2,1)S(1)}, u32[]{:S(2)}, u32[]{:S(2)}) collective-permute-start(bf16[64,256]{1,0:T(8,128)(2,1)S(1)} %constant_dynamic-update-slice_fusion), channel_id=1, source_target_pairs={{0,8},{1,9},{2,10},{3,11},{4,12},{5,13},{6,14},{7,15},{8,0},{9,1},... | collective-permute-start | bytes 98312 | tf_op jit(solution)/shard_map/ppermute | solution.py:19
  6.5 1.0 %copy-start = (bf16[64,2048]{1,0:T(8,128)(2,1)S(1)}, bf16[64,2048]{1,0:T(8,128)(2,1)}, u32[]{:S(2)}) copy-start(bf16[64,2048]{1,0:T(8,128)(2,1)} %q_ref.1) | copy-start | bytes 786436
  10.6 6.3 %collective-permute-start.4 = (bf16[256,256]{1,0:T(8,128)(2,1)S(1)}, bf16[256,256]{1,0:T(8,128)(2,1)S(1)}, u32[]{:S(2)}, u32[]{:S(2)}) collective-permute-start(bf16[256,256]{1,0:T(8,128)(2,1)S(1)} %pad_maximum_fusion.refs_2_), channel_id=1, source_target_pairs={{0,1},{1,0},{2,3},{3,2},{4,5},{5,4},{6,7},{7,6},{8,9},{9,8},{10,11... | collective-permute-start | bytes 393224 | tf_op jit(solution)/shard_map/ppermute | solution.py:19
  12.2 5.0 %collective-permute-start.5 = (bf16[256,256]{1,0:T(8,128)(2,1)S(1)}, bf16[256,256]{1,0:T(8,128)(2,1)S(1)}, u32[]{:S(2)}, u32[]{:S(2)}) collective-permute-start(bf16[256,256]{1,0:T(8,128)(2,1)S(1)} %pad_maximum_fusion.refs_2_), channel_id=1, source_target_pairs={{0,4},{1,5},{2,6},{3,7},{4,0},{5,1},{6,2},{7,3},{8,12},{9,13},{10,... | collective-permute-start | bytes 393224 | tf_op jit(solution)/shard_map/ppermute | solution.py:19
  13.7 5.9 %collective-permute-start.3 = (bf16[256,256]{1,0:T(8,128)(2,1)S(1)}, bf16[256,256]{1,0:T(8,128)(2,1)S(1)}, u32[]{:S(2)}, u32[]{:S(2)}) collective-permute-start(bf16[256,256]{1,0:T(8,128)(2,1)S(1)} %pad_maximum_fusion.refs_2_), channel_id=1, source_target_pairs={{0,5},{1,4},{2,7},{3,6},{4,1},{5,0},{6,3},{7,2},{8,13},{9,12},{10,... | collective-permute-start | bytes 393224 | tf_op jit(solution)/shard_map/ppermute | solution.py:19
  14.2 5.4 %collective-permute-start.7 = (bf16[256,256]{1,0:T(8,128)(2,1)S(1)}, bf16[256,256]{1,0:T(8,128)(2,1)S(1)}, u32[]{:S(2)}, u32[]{:S(2)}) collective-permute-start(bf16[256,256]{1,0:T(8,128)(2,1)S(1)} %pad_maximum_fusion.refs_2_), channel_id=1, source_target_pairs={{0,2},{1,3},{2,0},{3,1},{4,6},{5,7},{6,4},{7,5},{8,10},{9,11},{10,... | collective-permute-start | bytes 393224 | tf_op jit(solution)/shard_map/ppermute | solution.py:19
  16.9 2.7 %collective-permute-start.8 = (bf16[256,256]{1,0:T(8,128)(2,1)S(1)}, bf16[256,256]{1,0:T(8,128)(2,1)S(1)}, u32[]{:S(2)}, u32[]{:S(2)}) collective-permute-start(bf16[256,256]{1,0:T(8,128)(2,1)S(1)} %collective-permute-done.4.refs_2_), channel_id=1, source_target_pairs={{0,2},{1,3},{2,0},{3,1},{4,6},{5,7},{6,4},{7,5},{8,10},{9,11},{10,... | collective-permute-start | bytes 393224 | tf_op jit(solution)/shard_map/ppermute | solution.py:19
  17.2 2.4 %collective-permute-start.9 = (bf16[256,256]{1,0:T(8,128)(2,1)S(1)}, bf16[256,256]{1,0:T(8,128)(2,1)S(1)}, u32[]{:S(2)}, u32[]{:S(2)}) collective-permute-start(bf16[256,256]{1,0:T(8,128)(2,1)S(1)} %collective-permute-done.5.refs_3_), channel_id=1, source_target_pairs={{0,2},{1,3},{2,0},{3,1},{4,6},{5,7},{6,4},{7,5},{8,10},{9,11},{10,... | collective-permute-start | bytes 393224 | tf_op jit(solution)/shard_map/ppermute | solution.py:19
  19.6 2.1 %collective-permute-start.6 = (bf16[256,256]{1,0:T(8,128)(2,1)S(1)}, bf16[256,256]{1,0:T(8,128)(2,1)S(1)}, u32[]{:S(2)}, u32[]{:S(2)}) collective-permute-start(bf16[256,256]{1,0:T(8,128)(2,1)S(1)} %collective-permute-done.3.refs_5_), channel_id=1, source_target_pairs={{0,2},{1,3},{2,0},{3,1},{4,6},{5,7},{6,4},{7,5},{8,10},{9,11},{10,... | collective-permute-start | bytes 393224 | tf_op jit(solution)/shard_map/ppermute | solution.py:19
